TPU v7x, 768 devices: a whole 4x8x12 slice. The times are simulated.
768 devices in a mesh: dp: 24 (over z, x_hi), seq: 32 (over x_lo, y, core).
Axes of the slice: x: 4 (x_hi: 2, x_lo: 2; x = x_hi * 2 + x_lo), y: 8, z: 12, core: 2. Of those that a mesh axis runs over, the one named last changes fastest.
Arguments:
- query_rows: bfloat16 [98304, 2048], P(('dp', 'seq')), may hold values from -30 to 30, as said below
- key_rows: bfloat16 [98304, 2048], P(('dp', 'seq')), may hold values from -4 to 4
- value_rows: bfloat16 [98304, 2048], P(('dp', 'seq')), may hold values from -6 to 6
- clip_tiles: int32 [24, 32], P('dp'), may hold values from 0 to 3, never falling along the last dimension, each value on 1 to 16 neighbouring positions
- conditioning: bfloat16 [96, 3072], P(None, 'dp'), may hold values from -8 to 8
- gate_weight: bfloat16 [3072, 2048], P('dp', 'seq'), may hold values from -0.109375 to 0.109375
Outputs:
- attention_out: bfloat16 [98304, 2048], P(('dp', 'seq'))
Inputs may be any that keep to these rules, and one draw needn't show every extreme that they name: `query_rows`: entries of order one; a few rows are far larger. `clip_tiles`: clip numbers never fall along the tiles of a pack; every clip of 0 to 3 holds 1 to 16 tiles.
All inputs are finite; a program needn't handle non-finite values.
Results may differ from a plain program's by a relative error of at most 0.02.
Values may be sent and summed in bfloat16 or wider, within the bound.
A program may use at most 32 MiB of HBM per device.

v0:
```python
import math

import jax
import jax.numpy as jnp
from jax import lax
from jax.sharding import PartitionSpec as P

HD = 128
TILE = 128


def partner(x, axis, stride):
    return lax.ppermute(x, axis, [(i, i ^ 1 << stride) for i in range(lax.axis_size(axis))])


def blend(top_a, total_a, sum_a, top_b, total_b, sum_b):
    top_new = jnp.maximum(top_a, top_b)
    factor_a = jnp.exp(top_a - top_new)
    factor_b = jnp.exp(top_b - top_new)
    extra = (1,) * (sum_a.ndim - 2)
    weight_a = factor_a.reshape(factor_a.shape + extra)
    weight_b = factor_b.reshape(factor_b.shape + extra)
    return (top_new, total_a * factor_a + total_b * factor_b, sum_a * weight_a + sum_b * weight_b)


def attend_all(query_all, query_clips, key_all, key_clips, value_all, scale):
    row_count = query_all.shape[0]
    per_dev = query_all.shape[1]
    block = math.gcd(512, row_count)

    def attend(inputs):
        query_block, clip_block = inputs
        scores = (
            jnp.einsum("qhd,khd->hqk", query_block, key_all, preferred_element_type=jnp.float32)
            * scale
        )
        same = (clip_block[:, None] == key_clips[None, :])[None]
        masked = jnp.where(same, scores, -1e30)
        top = masked.max(axis=-1)
        weights = jnp.where(same, jnp.exp(masked - top[..., None]), 0.0)
        total = weights.sum(axis=-1)
        summed = jnp.einsum(
            "hqk,khd->qhd",
            weights.astype(jnp.bfloat16),
            value_all,
            preferred_element_type=jnp.float32,
        )
        return (top.T, total.T, summed)

    tops, totals, sums = lax.map(
        attend, (query_all.reshape(-1, block, per_dev, HD), query_clips.reshape(-1, block))
    )
    return (
        tops.reshape(row_count, per_dev),
        totals.reshape(row_count, per_dev),
        sums.reshape(row_count, per_dev, HD),
    )


def per_device(query_rows, key_rows, value_rows, clip_tiles, conditioning, gate_weight):
    seq_count = lax.axis_size("seq")
    tok_rows = query_rows.shape[0]
    width = query_rows.shape[1]
    head_total = width // HD
    per_dev = max(head_total // seq_count, 1)
    splits = max(seq_count // head_total, 1)
    groups = seq_count // splits
    group_cols = per_dev * HD
    own_cols = HD // splits
    part_rows = tok_rows // splits
    rows_all = seq_count * tok_rows
    scale = 1.0 / math.sqrt(HD)
    act = jax.nn.silu(conditioning.astype(jnp.float32)).astype(jnp.bfloat16)
    gate_part = jnp.dot(act, gate_weight, preferred_element_type=jnp.float32)
    gates = lax.psum_scatter(gate_part, "dp", scatter_dimension=0, tiled=True)

    def split_rows(array):
        return (
            array.reshape(splits, part_rows, groups, group_cols)
            .transpose(2, 0, 1, 3)
            .reshape(seq_count, part_rows, group_cols)
        )

    copies = jnp.broadcast_to(
        query_rows.reshape(tok_rows, groups, 1, group_cols), (tok_rows, groups, splits, group_cols)
    )
    query_send = copies.transpose(1, 2, 0, 3).reshape(seq_count, tok_rows, group_cols)
    key_send = split_rows(key_rows)
    value_send = split_rows(value_rows)
    query_got, key_got, value_got = (
        lax.all_to_all(query_send, "seq", split_axis=0, concat_axis=1, tiled=True),
        lax.all_to_all(key_send, "seq", split_axis=0, concat_axis=1, tiled=True),
        lax.all_to_all(value_send, "seq", split_axis=0, concat_axis=1, tiled=True),
    )
    query_got = query_got.reshape(-1, per_dev, HD)
    key_got = key_got.reshape(-1, per_dev, HD)
    value_got = value_got.reshape(-1, per_dev, HD)
    slot = lax.axis_index("seq") % splits
    token_clip = jnp.repeat(clip_tiles[0], TILE)
    part_pos = (
        jnp.arange(seq_count)[:, None] * tok_rows
        + slot * part_rows
        + jnp.arange(part_rows)[None, :]
    ).reshape(-1)
    part_clip = jnp.take(token_clip, part_pos)
    tops, totals, sums = attend_all(query_got, token_clip, key_got, part_clip, value_got, scale)
    other = (
        partner(tops.astype(jnp.bfloat16), "seq", 0).astype(tops.dtype),
        partner(totals.astype(jnp.bfloat16), "seq", 0).astype(totals.dtype),
        partner(sums.astype(jnp.bfloat16), "seq", 0).astype(sums.dtype),
    )
    tops, totals, sums = blend(tops, totals, sums, other[0], other[1], other[2])
    owned = lax.dynamic_slice_in_dim(sums, slot * own_cols, own_cols, 2)
    attended = (owned / totals[..., None]).reshape(rows_all, per_dev * own_cols)
    chooser = (token_clip[:, None] == jnp.arange(gates.shape[0])[None, :]).astype(jnp.float32)
    gate_rows = jnp.dot(
        chooser, gates, precision=lax.Precision.HIGHEST, preferred_element_type=jnp.float32
    )
    mixed = (attended * gate_rows).astype(jnp.bfloat16).reshape(seq_count, -1, attended.shape[1])
    returned = lax.all_to_all(mixed, "seq", split_axis=0, concat_axis=0, tiled=True)
    result = returned.transpose(1, 0, 2).reshape(tok_rows, width)
    return result


def solution(mesh):
    return jax.shard_map(
        per_device,
        mesh=mesh,
        in_specs=(
            P(("dp", "seq"), None),
            P(("dp", "seq"), None),
            P(("dp", "seq"), None),
            P("dp", None),
            P(None, "dp"),
            P("dp", "seq"),
        ),
        out_specs=P(("dp", "seq"), None),
        check_vma=False,
    )
```

profile of v0, /device:TPU:1, one launch (start us, length us, event | category | flops | bytes accessed | tf_op | source)
XLA Modules:
  0.0 275.5 jit_solution(14688695188865509080)
XLA Ops:
  0.0 1.2 copy.40
  1.2 0.9 copy.31
  2.1 14.1 %all-to-all-start.1 = ((bf16[32,64,128]{2,1,0:T(8,128)(2,1)}), bf16[32,64,128]{2,1,0:T(8,128)(2,1)S(1)}, u32[]{:S(2)}, u32[]{:S(2)}) async-start(bf16[32,64,128]{2,1,0:T(8,128)(2,1)} %bitcast.19), calls=%async_computation.1 | async-start | bytes 1048576 | tf_op jit(solution)/shard_map/all_to_all | solution.py:92
  16.2 0.0 copy-start.1
  16.2 1.2 copy.41
  17.4 0.9 copy.32
  18.3 14.6 %all-to-all-done.1 = bf16[32,64,128]{2,1,0:T(8,128)(2,1)S(1)} async-done(((bf16[32,64,128]{2,1,0:T(8,128)(2,1)}), bf16[32,64,128]{2,1,0:T(8,128)(2,1)S(1)}, u32[]{:S(2)}, u32[]{:S(2)}) %all-to-all-start.1) | async-done | bytes 524320 | tf_op jit(solution)/shard_map/all_to_all | solution.py:92
  32.9 5.6 %all-to-all-start.2 = ((bf16[32,64,128]{2,1,0:T(8,128)(2,1)}), bf16[32,64,128]{2,1,0:T(8,128)(2,1)S(1)}, u32[]{:S(2)}, u32[]{:S(2)}) async-start(bf16[32,64,128]{2,1,0:T(8,128)(2,1)} %bitcast.22), calls=%async_computation.2 | async-start | bytes 1048576 | tf_op jit(solution)/shard_map/all_to_all | solution.py:93
  38.6 0.1 copy_bitcast_fusion.1
  38.7 16.6 %all-to-all-done.2 = bf16[32,64,128]{2,1,0:T(8,128)(2,1)S(1)} async-done(((bf16[32,64,128]{2,1,0:T(8,128)(2,1)}), bf16[32,64,128]{2,1,0:T(8,128)(2,1)S(1)}, u32[]{:S(2)}, u32[]{:S(2)}) %all-to-all-start.2) | async-done | bytes 524320 | tf_op jit(solution)/shard_map/all_to_all | solution.py:93
  55.3 1.2 broadcast_in_dim.58
  56.5 5.7 %all-to-all-start = ((bf16[32,128,128]{2,1,0:T(8,128)(2,1)}), bf16[32,128,128]{2,1,0:T(8,128)(2,1)S(1)}, u32[]{:S(2)}, u32[]{:S(2)}) async-start(bf16[32,128,128]{2,1,0:T(8,128)(2,1)} %bitcast.15), calls=%async_computation | async-start | bytes 2097152 | tf_op jit(solution)/shard_map/all_to_all | solution.py:91
  62.2 0.1 iota_add_fusion
  62.3 0.1 add.92
  62.4 0.1 add.89
  62.4 0.6 broadcast.92
  63.0 0.7 reduce.7
  63.7 0.1 broadcast_in_dim.52
  63.8 0.1 copy.29
  63.9 0.1 broadcast_bitcast_fusion
  64.0 11.8 %gather_fusion = s32[2048]{0:T(1024)S(1)} fusion(s32[4096]{0:T(1024)S(1)} %broadcast_bitcast_fusion, s32[2048]{0:T(1024)S(1)} %broadcast_clamp_fusion), kind=kCustom, calls=%fused_computation | custom fusion | bytes 24576 | tf_op jit(solution)/shard_map/jit(_take)/gather | solution.py:105
  75.8 0.1 broadcast_bitcast_fusion.1
  75.9 12.8 %all-to-all-done = bf16[32,128,128]{2,1,0:T(8,128)(2,1)S(1)} async-done(((bf16[32,128,128]{2,1,0:T(8,128)(2,1)}), bf16[32,128,128]{2,1,0:T(8,128)(2,1)S(1)}, u32[]{:S(2)}, u32[]{:S(2)}) %all-to-all-start) | async-done | bytes 1048608 | tf_op jit(solution)/shard_map/all_to_all | solution.py:91
  88.7 32.5 %while.14 = (s32[]{:T(128)}, f32[8,512,1]{1,2,0:T(1,128)S(1)}, f32[8,512,1]{1,2,0:T(1,128)S(1)}, f32[8,512,1,128]{3,1,2,0:T(8,128)}, s32[8,512]{1,0:T(8,128)S(1)...) while((s32[]{:T(128)}, f32[8,512,1]{1,2,0:T(1,128)S(1)}, ...), condition=%wide.region_3.4_spmd, body=%wide.region_0.3_spmd.sunk | while | flops 553647104 | bytes 14076529 | solution.py:50
  88.7 0.9 fusion.49
  89.6 1.8 fusion.51
  91.5 1.2 fusion.50
  92.7 0.9 fusion.49
  93.7 1.8 fusion.51
  95.5 1.2 fusion.50
  96.8 0.9 fusion.49
  97.7 1.8 fusion.51
  99.6 1.2 fusion.50
  100.9 0.9 fusion.49
  101.8 1.8 fusion.51
  103.6 1.2 fusion.50
  104.9 0.9 fusion.49
  105.9 1.8 fusion.51
  107.7 1.2 fusion.50
  109.0 0.9 fusion.49
  109.9 1.8 fusion.51
  111.8 1.2 fusion.50
  113.1 0.9 fusion.49
  114.0 1.8 fusion.51
  115.8 1.2 fusion.50
  117.1 0.9 fusion.49
  118.0 1.8 fusion.51
  119.9 1.2 fusion.50
  121.2 0.0 copy-start.2
  121.2 0.0 copy-start.3
  121.2 1.9 copy.37
  123.1 1.1 convert_element_type.58
  124.2 4.1 %collective-permute-start.1 = (bf16[4096,1,128]{0,2,1:T(8,128)(2,1)}, bf16[4096,1,128]{0,2,1:T(8,128)(2,1)}, u32[]{:S(2)}, u32[]{:S(2)}) collective-permute-start(bf16[4096,1,128]{0,2,1:T(8,128)(2,1)} %convert_element_type.58), channel_id=1, source_target_pairs={{0,1},{1,0},{2,3},{3,2},{4,5},{5,4},{6,7},{7,6},{8,9},{9,8},{10,11... | collective-permute-start | bytes 3145736 | tf_op jit(solution)/shard_map/ppermute | solution.py:13
  128.4 0.1 fusion.30
  128.5 1.9 collective-permute-start
  130.5 2.4 collective-permute-start.2
  132.9 96.4 %all-reduce = f32[96,64]{1,0:T(8,128)S(1)} all-reduce(f32[96,64]{1,0:T(8,128)S(1)} %fusion.30), channel_id=2, replica_groups=mesh['dp'=24,'seq'=32] {'dp'}, use_global_device_ids=true, to_apply=%region_4.5.clone | all-reduce | flops 6144 | bytes 49152
  229.3 1.3 dynamic-slice
  231.2 0.0 collective-permute-done
  231.2 0.1 multiply_add_fusion
  231.3 1.8 fusion.21
  233.1 0.1 copy.44
  233.3 41.2 %all_to_all.32 = bf16[32,128,64]{1,2,0:T(8,128)(2,1)S(1)} all-to-all(bf16[32,128,64]{1,2,0:T(8,128)(2,1)S(1)} %bitcast.92), channel_id=1, replica_groups=mesh['dp'=24,'seq'=32] {'seq'}, dimensions={0} | all-to-all | bytes 1048576 | tf_op jit(solution)/shard_map/all_to_all | solution.py:120
  274.5 1.0 copy.36
  (32 shorter events, 0.2 us)
Async XLA Ops:
  0.0 38.6 %copy-start = (bf16[128,2048]{1,0:T(8,128)(2,1)S(1)}, bf16[128,2048]{1,0:T(8,128)(2,1)}, u32[]{:S(2)}) copy-start(bf16[128,2048]{1,0:T(8,128)(2,1)} %param.8) | copy-start | bytes 1572868
  2.1 30.8 %all-to-all-start.1 = ((bf16[32,64,128]{2,1,0:T(8,128)(2,1)}), bf16[32,64,128]{2,1,0:T(8,128)(2,1)S(1)}, u32[]{:S(2)}, u32[]{:S(2)}) async-start(bf16[32,64,128]{2,1,0:T(8,128)(2,1)} %bitcast.19), calls=%async_computation.1 | async-start | bytes 1048576 | tf_op jit(solution)/shard_map/all_to_all | solution.py:92
  16.2 46.8 %copy-start.1 = (s32[1,32]{1,0:T(1,128)S(1)}, s32[1,32]{1,0:T(1,128)}, u32[]{:S(2)}) copy-start(s32[1,32]{1,0:T(1,128)} %param.11) | copy-start | bytes 388
  32.9 22.4 %all-to-all-start.2 = ((bf16[32,64,128]{2,1,0:T(8,128)(2,1)}), bf16[32,64,128]{2,1,0:T(8,128)(2,1)S(1)}, u32[]{:S(2)}, u32[]{:S(2)}) async-start(bf16[32,64,128]{2,1,0:T(8,128)(2,1)} %bitcast.22), calls=%async_computation.2 | async-start | bytes 1048576 | tf_op jit(solution)/shard_map/all_to_all | solution.py:93
  56.5 32.1 %all-to-all-start = ((bf16[32,128,128]{2,1,0:T(8,128)(2,1)}), bf16[32,128,128]{2,1,0:T(8,128)(2,1)S(1)}, u32[]{:S(2)}, u32[]{:S(2)}) async-start(bf16[32,128,128]{2,1,0:T(8,128)(2,1)} %bitcast.15), calls=%async_computation | async-start | bytes 2097152 | tf_op jit(solution)/shard_map/all_to_all | solution.py:91
  121.2 7.2 %copy-start.2 = (bf16[96,128]{1,0:T(8,128)(2,1)S(1)}, bf16[96,128]{1,0:T(8,128)(2,1)}, u32[]{:S(2)}) copy-start(bf16[96,128]{1,0:T(8,128)(2,1)} %param.12) | copy-start | bytes 73732
  121.2 7.2 %copy-start.3 = (bf16[128,64]{0,1:T(8,128)(2,1)S(1)}, bf16[128,64]{0,1:T(8,128)(2,1)}, u32[]{:S(2)}) copy-start(bf16[128,64]{0,1:T(8,128)(2,1)} %param.13) | copy-start | bytes 49156
  124.2 107.1 %collective-permute-start.1 = (bf16[4096,1,128]{0,2,1:T(8,128)(2,1)}, bf16[4096,1,128]{0,2,1:T(8,128)(2,1)}, u32[]{:S(2)}, u32[]{:S(2)}) collective-permute-start(bf16[4096,1,128]{0,2,1:T(8,128)(2,1)} %convert_element_type.58), channel_id=1, source_target_pairs={{0,1},{1,0},{2,3},{3,2},{4,5},{5,4},{6,7},{7,6},{8,9},{9,8},{10,11... | collective-permute-start | bytes 3145736 | tf_op jit(solution)/shard_map/ppermute | solution.py:13
  128.5 102.7 %collective-permute-start = (bf16[4096,1]{0,1:T(2,128)(2,1)S(1)}, bf16[4096,1]{0,1:T(2,128)(2,1)S(1)}, u32[]{:S(2)}, u32[]{:S(2)}) collective-permute-start(bf16[4096,1]{0,1:T(2,128)(2,1)S(1)} %convert_element_type.56), channel_id=1, source_target_pairs={{0,1},{1,0},{2,3},{3,2},{4,5},{5,4},{6,7},{7,6},{8,9},{9,8},{10,11... | collective-permute-start | bytes 24584 | tf_op jit(solution)/shard_map/ppermute | solution.py:13
  130.5 100.7 %collective-permute-start.2 = (bf16[4096,1]{0,1:T(2,128)(2,1)S(1)}, bf16[4096,1]{0,1:T(2,128)(2,1)S(1)}, u32[]{:S(2)}, u32[]{:S(2)}) collective-permute-start(bf16[4096,1]{0,1:T(2,128)(2,1)S(1)} %convert_element_type.60), channel_id=1, source_target_pairs={{0,1},{1,0},{2,3},{3,2},{4,5},{5,4},{6,7},{7,6},{8,9},{9,8},{10,11... | collective-permute-start | bytes 24584 | tf_op jit(solution)/shard_map/ppermute | solution.py:13
where the time goes:
time: 276 us
  blocking collectives  138 us (50%)
  waiting for transfers between devices  44 us (16%)
  starting transfers between devices  33.8 us (12%)
  matrix products  24.1 us (9%)
  local copies, waits for them, and re-layouts  22.9 us (8%)
  other arithmetic  11.9 us (4%)
    unnamed x1, blocking collectives  96.4 us
    all_to_all x1, blocking collectives, per_device(): lax.all_to_all(mixed, 'seq', split_axis=0, concat_axis=0, tiled=True)  41.2 us
    all_to_all x1, waiting for transfers between devices, per_device(): lax.all_to_all(value_send, 'seq', split_axis=0, concat_axis=1, tiled=True)  16.6 us
    dot_general x8, matrix products, attend(): jnp.einsum('hqk,khd->qhd', weights.astype(jnp.bfloat16), value_all, prefe...  14.7 us
    all_to_all x1, waiting for transfers between devices, per_device(): lax.all_to_all(key_send, 'seq', split_axis=0, concat_axis=1, tiled=True)  14.6 us
    all_to_all x1, starting transfers between devices, per_device(): lax.all_to_all(key_send, 'seq', split_axis=0, concat_axis=1, tiled=True)  14.1 us
    all_to_all x1, waiting for transfers between devices, per_device(): lax.all_to_all(query_send, 'seq', split_axis=0, concat_axis=1, tiled=True)  12.8 us
    gather x1, local copies, waits for them, and re-layouts, per_device(): part_clip = jnp.take(token_clip, part_pos)  11.8 us
  transfers between devices with their start and end apart: 6, of which 3 were waited for; matrix products, arithmetic and copies ran while one was open for 6% of the time, Pallas kernels for 0%

commit v1 on v0

v1 whole, which is shorter than its diff:
```python
import functools
import math

import jax
import jax.numpy as jnp
from jax import lax
from jax.experimental import pallas as pl
from jax.experimental.pallas import tpu as pltpu
from jax.sharding import PartitionSpec as P

HD = 128
TILE = 128
CLIPS = 4
CHUNK = 2
LOG2E = 1.4426950408889634
MESH = pl.DeviceIdType.MESH


def remote(src, dst, send_sem, recv_sem, device):
    return pltpu.make_async_remote_copy(
        src_ref=src,
        dst_ref=dst,
        send_sem=send_sem,
        recv_sem=recv_sem,
        device_id=device,
        device_id_type=MESH,
    )


def columns(head):
    return pl.ds(pl.multiple_of(head * HD, HD), HD)


def place(chip, chips, step, sign):
    side = chips // 2
    turn = (step + 1) // 2
    far = (turn % 2) * ((turn + 1) // 2) + (1 - turn % 2) * (side - turn // 2)
    y = (chip % side + side + sign * (far % side)) % side
    x = (chip // side + (step + 1) % 2) % 2
    return x * side + y


def gather_kernel(
    chips,
    query_ref,
    key_ref,
    value_ref,
    query_out,
    key_out,
    value_out,
    query_send_sem,
    key_send_sem,
    value_send_sem,
    query_recv_sem,
    key_recv_sem,
    value_recv_sem,
    key_relay_send_sem,
    value_relay_send_sem,
    key_relay_recv_sem,
    value_relay_recv_sem,
    local_sem,
):
    seq = lax.axis_index("seq")
    chip = seq // 2
    core = seq % 2
    own_tile = seq
    partner = {"seq": 2 * chip + 1 - core}
    steps = chips - 1

    barrier = pltpu.get_barrier_semaphore()

    @pl.loop(1, chips)
    def _(k):
        other = {"seq": 2 * ((chip + k) % chips) + core}
        pl.semaphore_signal(barrier, inc=1, device_id=other, device_id_type=MESH)

    pl.semaphore_signal(barrier, inc=1, device_id=partner, device_id_type=MESH)

    own_key = pltpu.make_async_copy(
        key_ref.at[:, columns(chip)], key_out.at[own_tile], local_sem.at[0]
    )
    own_value = pltpu.make_async_copy(
        value_ref.at[:, columns(chip)], value_out.at[own_tile], local_sem.at[1]
    )
    own_query = pltpu.make_async_copy(
        query_ref.at[:, columns(chip)], query_out.at[chip], local_sem.at[2]
    )
    own_key.start()
    own_value.start()
    own_query.start()

    pl.semaphore_wait(barrier, chips)

    def shift(source, target, slot, send_sem, recv_sem, head):
        return remote(
            source.at[:, columns(head)],
            target.at[slot],
            send_sem.at[head],
            recv_sem.at[chip],
            {"seq": 2 * head + core},
        )

    def key_copy(head):
        return shift(key_ref, key_out, own_tile, key_send_sem, key_recv_sem, head)

    def value_copy(head):
        return shift(value_ref, value_out, own_tile, value_send_sem, value_recv_sem, head)

    def query_copy(head):
        return shift(query_ref, query_out, chip, query_send_sem, query_recv_sem, head)

    def relay(target, tile, send_sem, recv_sem):
        return remote(target.at[tile], target.at[tile], send_sem, recv_sem, partner)

    def key_relay(source):
        return relay(
            key_out,
            2 * source + core,
            key_relay_send_sem.at[source],
            key_relay_recv_sem.at[source],
        )

    def value_relay(source):
        return relay(
            value_out,
            2 * source + core,
            value_relay_send_sem.at[source],
            value_relay_recv_sem.at[source],
        )

    def arrived(buffer, slot, sem):
        remote(buffer.at[slot], buffer.at[slot], sem, sem, partner).wait_recv()

    @pl.loop(0, steps)
    def _(step):
        head = place(chip, chips, step, 1)
        key_copy(head).start()

    @pl.loop(0, steps)
    def _(step):
        head = place(chip, chips, step, 1)
        value_copy(head).start()

    @pl.loop(0, steps)
    def _(step):
        head = place(chip, chips, step, 1)
        query_copy(head).start()

    own_key.wait()
    key_relay(chip).start()
    own_value.wait()
    value_relay(chip).start()
    own_query.wait()

    @pl.loop(0, steps)
    def _(step):
        source = place(chip, chips, step, -1)
        arrived(key_out, 2 * source + core, key_recv_sem.at[source])
        key_relay(source).start()

    @pl.loop(0, steps)
    def _(step):
        source = place(chip, chips, step, -1)
        arrived(value_out, 2 * source + core, value_recv_sem.at[source])
        value_relay(source).start()

    @pl.loop(0, steps)
    def _(step):
        source = place(chip, chips, step, -1)
        arrived(query_out, source, query_recv_sem.at[source])
        head = place(chip, chips, step, 1)
        key_copy(head).wait_send()
        value_copy(head).wait_send()
        query_copy(head).wait_send()

    @pl.loop(0, chips)
    def _(source):
        tile = 2 * source + 1 - core
        arrived(key_out, tile, key_relay_recv_sem.at[source])
        arrived(value_out, tile, value_relay_recv_sem.at[source])
        key_relay(source).wait_send()
        value_relay(source).wait_send()


def attend_kernel(chips, most, clip_ref, query_ref, key_ref, value_ref, out_ref):
    core = lax.axis_index("seq") % 2
    tiles = 2 * chips

    def count(j, found):
        clip = clip_ref[0, j]
        return tuple(
            found[c] + jnp.where(clip < c + 1, 1, 0).astype(jnp.int32) for c in range(CLIPS - 1)
        )

    begins = lax.fori_loop(0, tiles, count, (jnp.int32(0),) * (CLIPS - 1))
    rate = LOG2E / math.sqrt(HD)
    ones = jnp.ones((CHUNK * TILE, HD), jnp.bfloat16)

    @pl.loop(0, chips)
    def _(source):
        clip = clip_ref[0, 2 * source + core]
        begin = jnp.int32(0)
        for c in range(1, CLIPS):
            begin = jnp.where(clip == c, begins[c - 1], begin)
        begin = jnp.minimum(begin, tiles - most)
        query = query_ref[source]
        scores = []
        top = None
        for j in range(most):
            score = lax.dot_general(
                query,
                key_ref[begin + j],
                (((1,), (1,)), ((), ())),
                preferred_element_type=jnp.float32,
            )
            score = score + jnp.where(clip_ref[0, begin + j] == clip, 0.0, -1e30)
            top = score if top is None else jnp.maximum(top, score)
            scores.append(score)
        top = jnp.max(top, axis=1, keepdims=True)
        summed = None
        for j in range(0, most, CHUNK):
            weights = jnp.concatenate(
                [jnp.exp2((scores[j + i] - top) * rate).astype(jnp.bfloat16) for i in range(CHUNK)],
                axis=1,
            )
            block = jnp.concatenate([value_ref[begin + j + i] for i in range(CHUNK)], axis=0)
            term = jnp.dot(
                weights,
                jnp.concatenate([block, ones], axis=1),
                preferred_element_type=jnp.float32,
            )
            summed = term if summed is None else summed + term
        out_ref[source] = summed[:, 0:HD] / summed[:, HD:]


def return_kernel(
    chips,
    clip_ref,
    attended_ref,
    gate_ref,
    out_ref,
    out_buf,
    land_buf,
    send_sem,
    recv_sem,
):
    seq = lax.axis_index("seq")
    chip = seq // 2
    core = seq % 2
    steps = chips - 1
    barrier = pltpu.get_barrier_semaphore()

    @pl.loop(1, chips)
    def _(k):
        other = {"seq": 2 * ((chip + k) % chips) + core}
        pl.semaphore_signal(barrier, inc=1, device_id=other, device_id_type=MESH)

    gates = gate_ref[...]

    def gated(source):
        clip = clip_ref[0, 2 * source + core]
        gate = gates[0:1, :]
        for c in range(1, CLIPS):
            gate = jnp.where(clip == c, gates[c : c + 1, :], gate)
        return (attended_ref[source] * gate).astype(jnp.bfloat16)

    @pl.loop(0, chips)
    def _(source):
        out_buf[source] = gated(source)

    pl.semaphore_wait(barrier, steps)

    def out_copy(other):
        return remote(
            out_buf.at[other],
            land_buf.at[chip],
            send_sem.at[other],
            recv_sem.at[chip],
            {"seq": 2 * other + core},
        )

    @pl.loop(0, steps)
    def _(step):
        other = place(chip, chips, step, -1)
        out_copy(other).start()

    out_ref[:, columns(chip)] = out_buf[chip]

    @pl.loop(0, steps)
    def _(step):
        other = place(chip, chips, step, -1)
        out_copy(other).wait_send()
        head = place(chip, chips, step, 1)
        remote(
            land_buf.at[head],
            land_buf.at[head],
            send_sem.at[head],
            recv_sem.at[head],
            {"seq": 2 * other + core},
        ).wait_recv()
        out_ref[:, columns(head)] = land_buf[head]


def per_device(query_rows, key_rows, value_rows, clip_tiles, conditioning, gate_weight):
    seq_count = lax.axis_size("seq")
    packs = lax.axis_size("dp")
    chips = seq_count // 2
    most = min(16, seq_count // 2)
    dma = pltpu.SemaphoreType.DMA
    vmem = pl.BlockSpec(memory_space=pltpu.VMEM)
    smem = pl.BlockSpec(memory_space=pltpu.SMEM)
    anywhere = pl.BlockSpec(memory_space=pl.ANY)

    act = jax.nn.silu(conditioning.astype(jnp.float32)).astype(jnp.bfloat16)
    part = jnp.dot(act, gate_weight, preferred_element_type=jnp.float32)
    parts = lax.all_to_all(part, "dp", split_axis=0, concat_axis=0, tiled=True)
    half = parts.reshape(packs, CLIPS, HD // 2).sum(axis=0)
    other_half = lax.ppermute(half, "seq", [(i, i ^ 1) for i in range(seq_count)])
    even = lax.axis_index("seq") % 2 == 0
    gates = jnp.concatenate(
        [jnp.where(even, half, other_half), jnp.where(even, other_half, half)], axis=1
    )

    query_all, key_all, value_all = pl.pallas_call(
        functools.partial(gather_kernel, chips),
        out_shape=[
            jax.ShapeDtypeStruct((chips, TILE, HD), jnp.bfloat16),
            jax.ShapeDtypeStruct((2 * chips, TILE, HD), jnp.bfloat16),
            jax.ShapeDtypeStruct((2 * chips, TILE, HD), jnp.bfloat16),
        ],
        in_specs=[anywhere] * 3,
        out_specs=[anywhere] * 3,
        scratch_shapes=[dma((chips,))] * 10 + [dma((3,))],
        compiler_params=pltpu.CompilerParams(
            collective_id=0, has_side_effects=True, vmem_limit_bytes=16 * 1024 * 1024
        ),
        cost_estimate=pl.CostEstimate(
            flops=0, bytes_accessed=200_000_000, transcendentals=0
        ),
        name="gather_heads",
    )(query_rows, key_rows, value_rows)

    attended = pl.pallas_call(
        functools.partial(attend_kernel, chips, most),
        out_shape=jax.ShapeDtypeStruct((chips, TILE, HD), jnp.float32),
        in_specs=[smem, vmem, vmem, vmem],
        out_specs=vmem,
        compiler_params=pltpu.CompilerParams(vmem_limit_bytes=40 * 1024 * 1024),
        cost_estimate=pl.CostEstimate(
            flops=4 * TILE * HD * TILE * most * chips,
            bytes_accessed=30_000_000,
            transcendentals=TILE * TILE * most * chips,
        ),
        name="attend",
    )(clip_tiles, query_all, key_all, value_all)

    return pl.pallas_call(
        functools.partial(return_kernel, chips),
        out_shape=jax.ShapeDtypeStruct(query_rows.shape, jnp.bfloat16),
        in_specs=[smem, vmem, vmem],
        out_specs=vmem,
        scratch_shapes=[
            pltpu.VMEM((chips, TILE, HD), jnp.bfloat16),
            pltpu.VMEM((chips, TILE, HD), jnp.bfloat16),
            dma((chips,)),
            dma((chips,)),
        ],
        compiler_params=pltpu.CompilerParams(
            collective_id=1, has_side_effects=True, vmem_limit_bytes=16 * 1024 * 1024
        ),
        name="return_tiles",
    )(clip_tiles, attended, gates)


def solution(mesh):
    return jax.shard_map(
        per_device,
        mesh=mesh,
        in_specs=(
            P(("dp", "seq"), None),
            P(("dp", "seq"), None),
            P(("dp", "seq"), None),
            P("dp", None),
            P(None, "dp"),
            P("dp", "seq"),
        ),
        out_specs=P(("dp", "seq"), None),
        check_vma=False,
    )
```

time: 276 us -> 113 us (0.41)
  blocking collectives: 138 us -> 0 us
  Pallas kernels: 0 us -> 78.3 us
  waiting for transfers between devices: 44 us -> 0.01 us
  matrix products: 24.1 us -> 0.88 us
  local copies, waits for them, and re-layouts: 22.9 us -> 8.5 us
  other arithmetic: 11.9 us -> 0.86 us
  starting transfers between devices: 33.8 us -> 24.3 us
    unnamed x1 -> x0, blocking collectives: 96.4 us -> none
    pallas_call x0 -> x3, Pallas kernels: none -> 78.3 us  [the longest x1 39.9 us: per_device(): pl.pallas_call(functools.partial(gather_kernel, chips), out_shape=[jax.Sh...]
    all_to_all x3 -> x1, waiting for transfers between devices: 44 us -> 0.01 us  [per_device(): parts = lax.all_to_all(part, 'dp', split_axis=0, concat_axis=0, tiled=True)]
    all_to_all x1 -> x0, blocking collectives: 41.2 us -> none  [per_device(): lax.all_to_all(mixed, 'seq', split_axis=0, concat_axis=0, tiled=True)]
    dot_general x18 -> x1, matrix products: 24.1 us -> 0.88 us  [per_device(): part = jnp.dot(act, gate_weight, preferred_element_type=jnp.float32)]
    gather x1 -> x0, local copies, waits for them, and re-layouts: 11.8 us -> none  [per_device(): part_clip = jnp.take(token_clip, part_pos)]
    reduce_sum x8 -> x1, other arithmetic: 9.96 us -> 0.04 us  [per_device(): half = parts.reshape(packs, CLIPS, HD // 2).sum(axis=0)]
    all_to_all x3 -> x1, starting transfers between devices: 25.3 us -> 18.4 us  [per_device(): parts = lax.all_to_all(part, 'dp', split_axis=0, concat_axis=0, tiled=True)]
  transfers between devices with their start and end apart: 6 -> 2, of which waited for: 3 -> 0; matrix products, arithmetic and copies ran while one was open for 6% -> 0% of each run, Pallas kernels for 0% -> 51%
where the time goes in v1:
time: 113 us
  Pallas kernels  78.3 us (69%)
  starting transfers between devices  24.3 us (22%)
  local copies, waits for them, and re-layouts  8.5 us (8%)
    pallas_call x1, Pallas kernels, per_device(): pl.pallas_call(functools.partial(gather_kernel, chips), out_shape=[jax.Sh...  39.9 us
    pallas_call x1, Pallas kernels, per_device(): pl.pallas_call(functools.partial(return_kernel, chips), out_shape=jax.Sha...  20.4 us
    all_to_all x1, starting transfers between devices, per_device(): parts = lax.all_to_all(part, 'dp', split_axis=0, concat_axis=0, tiled=True)  18.4 us
    pallas_call x1, Pallas kernels, per_device(): pl.pallas_call(functools.partial(attend_kernel, chips, most), out_shape=j...  18 us
    unnamed x17, local copies, waits for them, and re-layouts  7.91 us
    ppermute x1, starting transfers between devices, per_device(): lax.ppermute(half, 'seq', [(i, i ^ 1) for i in range(seq_count)])  5.88 us
  transfers between devices with their start and end apart: 2, of which 0 were waited for; matrix products, arithmetic and copies ran while one was open for 0% of the time, Pallas kernels for 51%

profile of v1, /device:TPU:1, one launch (start us, length us, event | category | flops | bytes accessed | tf_op | source)
XLA Modules:
  0.0 112.9 jit_solution(12749802621880725638)
XLA Ops:
  0.0 0.0 copy-start
  0.0 0.7 copy-done
  0.7 0.9 fusion.4
  1.6 0.7 reshape.4
  2.3 18.4 %all-to-all-start = ((f32[24,1,256]{2,1,0:T(1,128)}), f32[24,1,256]{2,1,0:T(1,128)S(1)}, u32[]{:S(2)}, u32[]{:S(2)}) async-start(f32[24,1,256]{2,1,0:T(1,128)} %reshape.4), calls=%async_computation | async-start | bytes 49152 | tf_op jit(solution)/shard_map/all_to_all | solution.py:316
  20.7 0.0 copy-start.1
  20.7 1.0 copy-done.1
  21.7 0.0 copy-start.2
  21.7 1.0 copy-done.2
  22.8 0.0 copy-start.3
  22.8 1.0 copy-done.3
  23.8 39.9 %gather_heads.1 = (bf16[16,128,128]{2,1,0:T(8,128)(2,1)S(1)}, bf16[32,128,128]{2,1,0:T(8,128)(2,1)S(1)}, bf16[32,128,128]{2,1,0:T(8,128)(2,1)S(1)}) custom-call(bf16[128,2048]{1,0:T(8,128)(2,1)S(1)} %copy-done.1, bf16[128,2048]{1,0:T(8,128)(2,1)S(1)} %copy-done.2, bf16[128,2048]{1,0:T(8,128)(2,1)S(1)} %copy-done.3), custom_call_target="tpu_custom_call" | custom-call | bytes 200000000 | tf_op jit(solution)/shard_map/gather_heads/pallas_call | solution.py:324
  63.8 0.0 copy-start.5
  63.8 0.8 copy-done.5
  64.6 0.0 all-to-all-done
  64.6 0.6 broadcast.3
  65.2 0.7 reduce.1
  65.9 0.1 reshape.5
  66.0 5.9 %collective-permute-start = (f32[4,64]{1,0:T(4,128)S(1)}, f32[4,64]{1,0:T(4,128)S(1)}, u32[]{:S(2)}, u32[]{:S(2)}) collective-permute-start(f32[4,64]{1,0:T(4,128)S(1)} %reduce_sum.9), channel_id=1, source_target_pairs={{0,1},{1,0},{2,3},{3,2},{4,5},{5,4},{6,7},{7,6},{8,9},{9,8},{10,11... | collective-permute-start | bytes 3080 | tf_op jit(solution)/shard_map/ppermute | solution.py:318
  71.9 0.0 copy-start.4
  71.9 0.6 copy-done.4
  72.6 0.0 copy-start.6
  72.6 1.0 copy-done.6
  73.6 18.0 %attend.1.attended_ref = f32[16,128,128]{2,1,0:T(8,128)S(1)} custom-call(s32[1,32]{1,0:T(1,128)S(1)} %copy-done.4, bf16[16,128,128]{2,1,0:T(8,128)(2,1)S(1)} %copy-done.6, bf16[32,128,128]{2,1,0:T(8,128)(2,1)S(1)} %get-tuple-element.9.key_ref, bf16[32,128,128]{2,1,0:T(8,128)(2,1)S(1)} %get-tuple-element.10.value_ref), custom_call_target="tpu_custom_call" | custom-call | flops 2147483648 | bytes 30000000 | tf_op jit(solution)/shard_map/attend/pallas_call | solution.py:343
  91.7 0.0 collective-permute-done
  91.7 0.1 pad_maximum_fusion.gate_ref
  91.8 20.4 %return_tiles.1 = bf16[128,2048]{1,0:T(8,128)(2,1)S(1)} custom-call(s32[1,32]{1,0:T(1,128)S(1)} %copy-done.4, f32[16,128,128]{2,1,0:T(8,128)S(1)} %attend.1.attended_ref, f32[4,128]{1,0:T(4,128)S(1)} %pad_maximum_fusion.gate_ref), custom_call_target="tpu_custom_call" | custom-call | tf_op jit(solution)/shard_map/return_tiles/pallas_call | solution.py:357
  112.1 0.8 copy.10
  (2 shorter events, 0.0 us)
Async XLA Ops:
  0.0 0.7 copy-start
  2.3 62.3 %all-to-all-start = ((f32[24,1,256]{2,1,0:T(1,128)}), f32[24,1,256]{2,1,0:T(1,128)S(1)}, u32[]{:S(2)}, u32[]{:S(2)}) async-start(f32[24,1,256]{2,1,0:T(1,128)} %reshape.4), calls=%async_computation | async-start | bytes 49152 | tf_op jit(solution)/shard_map/all_to_all | solution.py:316
  20.7 1.0 copy-start.1
  21.7 1.0 copy-start.2
  22.8 1.0 copy-start.3
  63.8 0.8 copy-start.5
  66.0 25.6 %collective-permute-start = (f32[4,64]{1,0:T(4,128)S(1)}, f32[4,64]{1,0:T(4,128)S(1)}, u32[]{:S(2)}, u32[]{:S(2)}) collective-permute-start(f32[4,64]{1,0:T(4,128)S(1)} %reduce_sum.9), channel_id=1, source_target_pairs={{0,1},{1,0},{2,3},{3,2},{4,5},{5,4},{6,7},{7,6},{8,9},{9,8},{10,11... | collective-permute-start | bytes 3080 | tf_op jit(solution)/shard_map/ppermute | solution.py:318
  71.9 0.7 copy-start.4
  72.6 1.0 copy-start.6

commit v2 on v1

--- a/solution.py
+++ b/solution.py
@@ -12,6 +12,8 @@
 TILE = 128
 CLIPS = 4
 CHUNK = 2
+GROUP = 4
+ATTEND_VMEM = 60
 LOG2E = 1.4426950408889634
 MESH = pl.DeviceIdType.MESH
 
@@ -182,10 +184,70 @@
         value_relay(source).wait_send()
 
 
-def attend_kernel(chips, most, clip_ref, query_ref, key_ref, value_ref, out_ref):
-    core = lax.axis_index("seq") % 2
+def gate_kernel(packs, cond_ref, weight_ref, half_ref, send_buf, recv_buf, send_sem, recv_sem):
+    pack = lax.axis_index("dp")
+    barrier = pltpu.get_barrier_semaphore()
+
+    @pl.loop(1, packs)
+    def _(k):
+        other = {"dp": (pack + k) % packs}
+        pl.semaphore_signal(barrier, inc=1, device_id=other, device_id_type=MESH)
+
+    cond = cond_ref[...].astype(jnp.float32)
+    act = (cond / (1.0 + jnp.exp(-cond))).astype(jnp.bfloat16)
+    part = jnp.dot(act, weight_ref[...], preferred_element_type=jnp.float32)
+    send_buf[...] = jnp.zeros_like(send_buf)
+    for p in range(packs):
+        send_buf[p, 0:CLIPS, 0 : HD // 2] = part[p * CLIPS : (p + 1) * CLIPS, :]
+    recv_buf[pack] = send_buf[pack]
+
+    pl.semaphore_wait(barrier, packs - 1)
+
+    def gate_copy(other):
+        return remote(
+            send_buf.at[other],
+            recv_buf.at[pack],
+            send_sem.at[other],
+            recv_sem.at[pack],
+            {"dp": other},
+        )
+
+    @pl.loop(1, packs)
+    def _(k):
+        gate_copy((pack + k) % packs).start()
+
+    @pl.loop(1, packs)
+    def _(k):
+        source = (pack + packs - k) % packs
+        remote(
+            recv_buf.at[source],
+            recv_buf.at[source],
+            send_sem.at[source],
+            recv_sem.at[source],
+            {"dp": source},
+        ).wait_recv()
+
+    half_ref[...] = jnp.sum(recv_buf[...], axis=0)
+
+    @pl.loop(1, packs)
+    def _(k):
+        gate_copy((pack + k) % packs).wait_send()
+
+
+def attend_kernel(
+    chips,
+    most,
+    clip_ref,
+    query_buf,
+    key_buf,
+    value_buf,
+    half_ref,
+    other_ref,
+    out_ref,
+):
+    seq = lax.axis_index("seq")
+    core = seq % 2
     tiles = 2 * chips
-
     def count(j, found):
         clip = clip_ref[0, j]
         return tuple(
@@ -196,57 +258,66 @@
     rate = LOG2E / math.sqrt(HD)
     ones = jnp.ones((CHUNK * TILE, HD), jnp.bfloat16)
 
-    @pl.loop(0, chips)
-    def _(source):
+    half = half_ref[:, 0 : HD // 2]
+    other_half = other_ref[:, 0 : HD // 2]
+    gates = jnp.where(
+        core == 0,
+        jnp.concatenate([half, other_half], axis=1),
+        jnp.concatenate([other_half, half], axis=1),
+    )
+
+    def weigh(source):
         clip = clip_ref[0, 2 * source + core]
         begin = jnp.int32(0)
+        gate = gates[0:1, :]
         for c in range(1, CLIPS):
             begin = jnp.where(clip == c, begins[c - 1], begin)
+            gate = jnp.where(clip == c, gates[c : c + 1, :], gate)
         begin = jnp.minimum(begin, tiles - most)
-        query = query_ref[source]
+        query = query_buf[source]
         scores = []
-        top = None
-        for j in range(most):
+        for j in range(0, most, CHUNK):
+            block = jnp.concatenate([key_buf[begin + j + i] for i in range(CHUNK)], axis=0)
             score = lax.dot_general(
-                query,
-                key_ref[begin + j],
-                (((1,), (1,)), ((), ())),
-                preferred_element_type=jnp.float32,
+                query, block, (((1,), (1,)), ((), ())), preferred_element_type=jnp.float32
             )
-            score = score + jnp.where(clip_ref[0, begin + j] == clip, 0.0, -1e30)
-            top = score if top is None else jnp.maximum(top, score)
-            scores.append(score)
-        top = jnp.max(top, axis=1, keepdims=True)
+            for i in range(CHUNK):
+                hide = jnp.where(clip_ref[0, begin + j + i] == clip, 0.0, -1e30)
+                scores.append(score[:, i * TILE : (i + 1) * TILE] + hide)
+        tops = scores
+        while len(tops) > 1:
+            tops = [jnp.maximum(a, b) for a, b in zip(tops[0::2], tops[1::2])]
+        return begin, gate, scores, jnp.max(tops[0], axis=1, keepdims=True)
+
+    def mix(slot, begin, gate, scores, top):
         summed = None
         for j in range(0, most, CHUNK):
             weights = jnp.concatenate(
                 [jnp.exp2((scores[j + i] - top) * rate).astype(jnp.bfloat16) for i in range(CHUNK)],
                 axis=1,
             )
-            block = jnp.concatenate([value_ref[begin + j + i] for i in range(CHUNK)], axis=0)
+            block = jnp.concatenate([value_buf[begin + j + i] for i in range(CHUNK)], axis=0)
             term = jnp.dot(
                 weights,
                 jnp.concatenate([block, ones], axis=1),
                 preferred_element_type=jnp.float32,
             )
             summed = term if summed is None else summed + term
-        out_ref[source] = summed[:, 0:HD] / summed[:, HD:]
-
-
-def return_kernel(
-    chips,
-    clip_ref,
-    attended_ref,
-    gate_ref,
-    out_ref,
-    out_buf,
-    land_buf,
-    send_sem,
-    recv_sem,
-):
+        out_ref[slot] = (summed[:, 0:HD] / summed[:, HD:] * gate).astype(jnp.bfloat16)
+
+    @pl.loop(0, chips // GROUP)
+    def _(group):
+        slots = [group * GROUP + i for i in range(GROUP)]
+        states = [weigh(slot) for slot in slots]
+        for slot, state in zip(slots, states):
+            mix(slot, *state)
+
+
+def return_kernel(chips, attended_ref, out_ref, land_buf, send_sem, recv_sem, local_sem):
     seq = lax.axis_index("seq")
     chip = seq // 2
     core = seq % 2
+    partner = {"seq": 2 * chip + 1 - core}
     steps = chips - 1
     barrier = pltpu.get_barrier_semaphore()
 
@@ -255,24 +326,14 @@
         other = {"seq": 2 * ((chip + k) % chips) + core}
         pl.semaphore_signal(barrier, inc=1, device_id=other, device_id_type=MESH)
 
-    gates = gate_ref[...]
-
-    def gated(source):
-        clip = clip_ref[0, 2 * source + core]
-        gate = gates[0:1, :]
-        for c in range(1, CLIPS):
-            gate = jnp.where(clip == c, gates[c : c + 1, :], gate)
-        return (attended_ref[source] * gate).astype(jnp.bfloat16)
-
-    @pl.loop(0, chips)
-    def _(source):
-        out_buf[source] = gated(source)
+    own = pltpu.make_async_copy(attended_ref.at[chip], land_buf.at[chip], local_sem)
+    own.start()
 
     pl.semaphore_wait(barrier, steps)
 
     def out_copy(other):
         return remote(
-            out_buf.at[other],
+            attended_ref.at[other],
             land_buf.at[chip],
             send_sem.at[other],
             recv_sem.at[chip],
@@ -281,24 +342,26 @@
 
     @pl.loop(0, steps)
     def _(step):
-        other = place(chip, chips, step, -1)
-        out_copy(other).start()
-
-    out_ref[:, columns(chip)] = out_buf[chip]
-
-    @pl.loop(0, steps)
-    def _(step):
-        other = place(chip, chips, step, -1)
-        out_copy(other).wait_send()
-        head = place(chip, chips, step, 1)
+        out_copy(place(chip, chips, chips - 2 - step, -1)).start()
+
+    own.wait()
+    out_ref[:, columns(chip)] = land_buf[chip]
+
+    @pl.loop(0, steps)
+    def _(step):
+        head = place(chip, chips, chips - 2 - step, 1)
         remote(
             land_buf.at[head],
             land_buf.at[head],
             send_sem.at[head],
             recv_sem.at[head],
-            {"seq": 2 * other + core},
+            partner,
         ).wait_recv()
         out_ref[:, columns(head)] = land_buf[head]
+
+    @pl.loop(0, steps)
+    def _(step):
+        out_copy(place(chip, chips, step, -1)).wait_send()
 
 
 def per_device(query_rows, key_rows, value_rows, clip_tiles, conditioning, gate_weight):
@@ -310,66 +373,59 @@
     vmem = pl.BlockSpec(memory_space=pltpu.VMEM)
     smem = pl.BlockSpec(memory_space=pltpu.SMEM)
     anywhere = pl.BlockSpec(memory_space=pl.ANY)
-
-    act = jax.nn.silu(conditioning.astype(jnp.float32)).astype(jnp.bfloat16)
-    part = jnp.dot(act, gate_weight, preferred_element_type=jnp.float32)
-    parts = lax.all_to_all(part, "dp", split_axis=0, concat_axis=0, tiled=True)
-    half = parts.reshape(packs, CLIPS, HD // 2).sum(axis=0)
-    other_half = lax.ppermute(half, "seq", [(i, i ^ 1) for i in range(seq_count)])
-    even = lax.axis_index("seq") % 2 == 0
-    gates = jnp.concatenate(
-        [jnp.where(even, half, other_half), jnp.where(even, other_half, half)], axis=1
-    )
+    part_shape = jax.ShapeDtypeStruct((chips, TILE, HD), jnp.bfloat16)
+    whole_shape = jax.ShapeDtypeStruct((2 * chips, TILE, HD), jnp.bfloat16)
+
+    half = pl.pallas_call(
+        functools.partial(gate_kernel, packs),
+        out_shape=jax.ShapeDtypeStruct((8, HD), jnp.float32),
+        in_specs=[vmem, vmem],
+        out_specs=vmem,
+        scratch_shapes=[
+            pltpu.VMEM((packs, 8, HD), jnp.float32),
+            pltpu.VMEM((packs, 8, HD), jnp.float32),
+            dma((packs,)),
+            dma((packs,)),
+        ],
+        compiler_params=pltpu.CompilerParams(collective_id=2, has_side_effects=True),
+        name="sum_gates",
+    )(conditioning, gate_weight)
+
+    other = lax.ppermute(half, "seq", [(i, i ^ 1) for i in range(seq_count)])
 
     query_all, key_all, value_all = pl.pallas_call(
         functools.partial(gather_kernel, chips),
-        out_shape=[
-            jax.ShapeDtypeStruct((chips, TILE, HD), jnp.bfloat16),
-            jax.ShapeDtypeStruct((2 * chips, TILE, HD), jnp.bfloat16),
-            jax.ShapeDtypeStruct((2 * chips, TILE, HD), jnp.bfloat16),
-        ],
+        out_shape=[part_shape, whole_shape, whole_shape],
         in_specs=[anywhere] * 3,
         out_specs=[anywhere] * 3,
         scratch_shapes=[dma((chips,))] * 10 + [dma((3,))],
-        compiler_params=pltpu.CompilerParams(
-            collective_id=0, has_side_effects=True, vmem_limit_bytes=16 * 1024 * 1024
-        ),
-        cost_estimate=pl.CostEstimate(
-            flops=0, bytes_accessed=200_000_000, transcendentals=0
-        ),
+        compiler_params=pltpu.CompilerParams(collective_id=0, has_side_effects=True),
         name="gather_heads",
     )(query_rows, key_rows, value_rows)
 
     attended = pl.pallas_call(
         functools.partial(attend_kernel, chips, most),
-        out_shape=jax.ShapeDtypeStruct((chips, TILE, HD), jnp.float32),
-        in_specs=[smem, vmem, vmem, vmem],
+        out_shape=part_shape,
+        in_specs=[smem, vmem, vmem, vmem, vmem, vmem],
         out_specs=vmem,
-        compiler_params=pltpu.CompilerParams(vmem_limit_bytes=40 * 1024 * 1024),
-        cost_estimate=pl.CostEstimate(
-            flops=4 * TILE * HD * TILE * most * chips,
-            bytes_accessed=30_000_000,
-            transcendentals=TILE * TILE * most * chips,
-        ),
+        compiler_params=pltpu.CompilerParams(vmem_limit_bytes=ATTEND_VMEM * 1024 * 1024),
         name="attend",
-    )(clip_tiles, query_all, key_all, value_all)
+    )(clip_tiles, query_all, key_all, value_all, half, other)
 
     return pl.pallas_call(
         functools.partial(return_kernel, chips),
         out_shape=jax.ShapeDtypeStruct(query_rows.shape, jnp.bfloat16),
-        in_specs=[smem, vmem, vmem],
+        in_specs=[anywhere],
         out_specs=vmem,
         scratch_shapes=[
             pltpu.VMEM((chips, TILE, HD), jnp.bfloat16),
-            pltpu.VMEM((chips, TILE, HD), jnp.bfloat16),
             dma((chips,)),
             dma((chips,)),
+            dma,
         ],
-        compiler_params=pltpu.CompilerParams(
-            collective_id=1, has_side_effects=True, vmem_limit_bytes=16 * 1024 * 1024
-        ),
+        compiler_params=pltpu.CompilerParams(collective_id=1, has_side_effects=True),
         name="return_tiles",
-    )(clip_tiles, attended, gates)
+    )(attended)
 
 
 def solution(mesh):

time: 113 us -> 107 us (0.947)
  Pallas kernels: 78.3 us -> 99.2 us
  starting transfers between devices: 24.3 us -> 3.75 us
  local copies, waits for them, and re-layouts: 8.5 us -> 3.9 us
    pallas_call x2 -> x3, Pallas kernels: 58 us -> 77.2 us  [the longest x1 42.2 us: per_device(): pl.pallas_call(functools.partial(gather_kernel, chips), out_shape=[part_s...]
    all_to_all x1 -> x0, starting transfers between devices: 18.4 us -> none  [per_device(): parts = lax.all_to_all(part, 'dp', split_axis=0, concat_axis=0, tiled=True)]
    unnamed x17 -> x4, local copies, waits for them, and re-layouts: 7.91 us -> 3.9 us
    ppermute x1, starting transfers between devices: 5.88 us -> 3.75 us  [per_device(): other = lax.ppermute(half, 'seq', [(i, i ^ 1) for i in range(seq_count)])]
    pallas_call x1, Pallas kernels: 20.4 us -> 22 us  [per_device(): pl.pallas_call(functools.partial(return_kernel, chips), out_shape=jax.Sha...]
  transfers between devices with their start and end apart: 2 -> 1, of which waited for: 0 -> 0; matrix products, arithmetic and copies ran while one was open for 0% -> 0% of each run, Pallas kernels for 51% -> 39%
where the time goes in v2:
time: 107 us
  Pallas kernels  99.2 us (93%)
  local copies, waits for them, and re-layouts  3.9 us (4%)
  starting transfers between devices  3.75 us (4%)
    pallas_call x1, Pallas kernels, per_device(): pl.pallas_call(functools.partial(gather_kernel, chips), out_shape=[part_s...  42.2 us
    pallas_call x1, Pallas kernels, per_device(): pl.pallas_call(functools.partial(gate_kernel, packs), out_shape=jax.Shape...  26.3 us
    pallas_call x1, Pallas kernels, per_device(): pl.pallas_call(functools.partial(return_kernel, chips), out_shape=jax.Sha...  22 us
    pallas_call x1, Pallas kernels, per_device(): pl.pallas_call(functools.partial(attend_kernel, chips, most), out_shape=p...  8.7 us
    unnamed x4, local copies, waits for them, and re-layouts  3.9 us
    ppermute x1, starting transfers between devices, per_device(): other = lax.ppermute(half, 'seq', [(i, i ^ 1) for i in range(seq_count)])  3.75 us
  transfers between devices with their start and end apart: 1, of which 0 were waited for; matrix products, arithmetic and copies ran while one was open for 0% of the time, Pallas kernels for 39%

profile of v2, /device:TPU:1, one launch (start us, length us, event | category | flops | bytes accessed | tf_op | source)
XLA Modules:
  0.0 106.9 jit_solution(9185713599105554325)
XLA Ops:
  0.0 1.4 %copy.7.weight_ref = bf16[128,64]{1,0:T(8,128)(2,1)} copy(bf16[128,64]{0,1:T(8,128)(2,1)} %param.11) | data formatting | bytes 32768 | tf_op args[5]
  1.4 26.3 %sum_gates.1.half_ref = f32[8,128]{1,0:T(8,128)} custom-call(bf16[96,128]{1,0:T(8,128)(2,1)} %cond_ref.1, bf16[128,64]{1,0:T(8,128)(2,1)} %copy.7.weight_ref), custom_call_target="tpu_custom_call" | custom-call | tf_op jit(solution)/shard_map/sum_gates/pallas_call | solution.py:379
  27.8 3.8 %collective-permute-start = (f32[8,128]{1,0:T(8,128)}, f32[8,128]{1,0:T(8,128)S(1)}, u32[]{:S(2)}, u32[]{:S(2)}) collective-permute-start(f32[8,128]{1,0:T(8,128)} %sum_gates.1.half_ref), channel_id=1, source_target_pairs={{0,1},{1,0},{2,3},{3,2},{4,5},{5,4},{6,7},{7,6},{8,9},{9,8},{10,11... | collective-permute-start | bytes 12296 | tf_op jit(solution)/shard_map/ppermute | solution.py:394
  31.5 42.2 %gather_heads.1 = (bf16[16,128,128]{2,1,0:T(8,128)(2,1)}, bf16[32,128,128]{2,1,0:T(8,128)(2,1)}, bf16[32,128,128]{2,1,0:T(8,128)(2,1)}) custom-call(bf16[128,2048]{1,0:T(8,128)(2,1)} %query_ref.1, bf16[128,2048]{1,0:T(8,128)(2,1)} %key_ref.1, bf16[128,2048]{1,0:T(8,128)(2,1)} %value_ref.1), custom_call_target="tpu_custom_call" | custom-call | tf_op jit(solution)/shard_map/gather_heads/pallas_call | solution.py:396
  73.7 0.0 collective-permute-done.other_ref
  73.7 0.0 copy-start
  73.7 0.6 copy-done
  74.3 8.7 %attend.1.attended_ref = bf16[16,128,128]{2,1,0:T(8,128)(2,1)} custom-call(s32[1,32]{1,0:T(1,128)} %clip_ref.1, bf16[16,128,128]{2,1,0:T(8,128)(2,1)} %get-tuple-element.8.query_buf, bf16[32,128,128]{2,1,0:T(8,128)(2,1)} %get-tuple-element.9.key_buf, bf16[32,128,128]{2,1,0:T(8,128)(2,1)} %get-tuple-element.10.value_buf, f32[8,128]{1,0:T(8,128)} %sum_gates.1.half_ref, ...), custom_call_target="tpu_custom_call" | custom-call | tf_op jit(solution)/shard_map/attend/pallas_call | solution.py:406
  83.0 22.0 %return_tiles.1 = bf16[128,2048]{1,0:T(8,128)(2,1)} custom-call(bf16[16,128,128]{2,1,0:T(8,128)(2,1)} %attend.1.attended_ref), custom_call_target="tpu_custom_call" | custom-call | tf_op jit(solution)/shard_map/return_tiles/pallas_call | solution.py:415
  105.1 1.9 %copy.9 = bf16[128,2048]{1,0:T(8,128)(2,1)} copy(bf16[128,2048]{1,0:T(8,128)(2,1)} %return_tiles.1) | data formatting | bytes 1048576
Async XLA Ops:
  27.8 45.9 %collective-permute-start = (f32[8,128]{1,0:T(8,128)}, f32[8,128]{1,0:T(8,128)S(1)}, u32[]{:S(2)}, u32[]{:S(2)}) collective-permute-start(f32[8,128]{1,0:T(8,128)} %sum_gates.1.half_ref), channel_id=1, source_target_pairs={{0,1},{1,0},{2,3},{3,2},{4,5},{5,4},{6,7},{7,6},{8,9},{9,8},{10,11... | collective-permute-start | bytes 12296 | tf_op jit(solution)/shard_map/ppermute | solution.py:394
  73.7 0.6 copy-start

commit v3 on v2

--- a/solution.py
+++ b/solution.py
@@ -33,23 +33,34 @@
     return pl.ds(pl.multiple_of(head * HD, HD), HD)
 
 
-def place(chip, chips, step, sign):
+def others(chip, chips, sign):
     side = chips // 2
-    turn = (step + 1) // 2
-    far = (turn % 2) * ((turn + 1) // 2) + (1 - turn % 2) * (side - turn // 2)
-    y = (chip % side + side + sign * (far % side)) % side
-    x = (chip // side + (step + 1) % 2) % 2
-    return x * side + y
+    x, y = lax.div(chip, side), lax.rem(chip, side)
+    found = []
+    for turn in range(side):
+        far = (turn + 1) // 2 if turn % 2 else (side - turn // 2) % side
+        row = lax.rem(y + (far if sign > 0 else side - far), side)
+        for cross in range(2):
+            if turn or cross:
+                found.append(lax.rem(x + cross, 2) * side + row)
+    return found
 
 
 def gather_kernel(
     chips,
+    packs,
     query_ref,
     key_ref,
     value_ref,
+    cond_ref,
+    weight_ref,
     query_out,
     key_out,
     value_out,
+    gate_out,
+    gate_send,
+    gate_recv,
+    gate_half,
     query_send_sem,
     key_send_sem,
     value_send_sem,
@@ -61,22 +72,30 @@
     key_relay_recv_sem,
     value_relay_recv_sem,
     local_sem,
+    gate_send_sem,
+    gate_recv_sem,
+    half_send_sem,
+    half_recv_sem,
 ):
+    pack = lax.axis_index("dp")
     seq = lax.axis_index("seq")
-    chip = seq // 2
-    core = seq % 2
+    chip = lax.div(seq, 2)
+    core = lax.rem(seq, 2)
     own_tile = seq
     partner = {"seq": 2 * chip + 1 - core}
-    steps = chips - 1
+    ahead = others(chip, chips, 1)
+    behind = others(chip, chips, -1)
+    packs_ahead = [lax.rem(pack + k, packs) for k in range(1, packs)]
 
     barrier = pltpu.get_barrier_semaphore()
 
-    @pl.loop(1, chips)
-    def _(k):
-        other = {"seq": 2 * ((chip + k) % chips) + core}
+    for head in ahead:
+        other = {"seq": 2 * head + core}
         pl.semaphore_signal(barrier, inc=1, device_id=other, device_id_type=MESH)
 
     pl.semaphore_signal(barrier, inc=1, device_id=partner, device_id_type=MESH)
+    for other in packs_ahead:
+        pl.semaphore_signal(barrier, inc=1, device_id={"dp": other}, device_id_type=MESH)
 
     own_key = pltpu.make_async_copy(
         key_ref.at[:, columns(chip)], key_out.at[own_tile], local_sem.at[0]
@@ -91,7 +110,17 @@
     own_value.start()
     own_query.start()
 
-    pl.semaphore_wait(barrier, chips)
+    cond = cond_ref[...].astype(jnp.float32)
+    act = (cond / (1.0 + jnp.exp(-cond))).astype(jnp.bfloat16)
+    part = lax.dot_general(
+        act, weight_ref[...], (((1,), (1,)), ((), ())), preferred_element_type=jnp.float32
+    )
+    gate_send[...] = jnp.zeros_like(gate_send)
+    for p in range(packs):
+        gate_send[p, 0:CLIPS, 0 : HD // 2] = part[p * CLIPS : (p + 1) * CLIPS, :]
+    gate_recv[pack] = gate_send[pack]
+
+    pl.semaphore_wait(barrier, chips + packs - 1)
 
     def shift(source, target, slot, send_sem, recv_sem, head):
         return remote(
@@ -133,105 +162,66 @@
     def arrived(buffer, slot, sem):
         remote(buffer.at[slot], buffer.at[slot], sem, sem, partner).wait_recv()
 
-    @pl.loop(0, steps)
-    def _(step):
-        head = place(chip, chips, step, 1)
+    def gate_copy(other):
+        return remote(
+            gate_send.at[other],
+            gate_recv.at[pack],
+            gate_send_sem.at[other],
+            gate_recv_sem.at[pack],
+            {"dp": other},
+        )
+
+    for head in ahead:
         key_copy(head).start()
-
-    @pl.loop(0, steps)
-    def _(step):
-        head = place(chip, chips, step, 1)
-        value_copy(head).start()
-
-    @pl.loop(0, steps)
-    def _(step):
-        head = place(chip, chips, step, 1)
-        query_copy(head).start()
-
     own_key.wait()
     key_relay(chip).start()
+    for head in ahead:
+        value_copy(head).start()
     own_value.wait()
     value_relay(chip).start()
-    own_query.wait()
-
-    @pl.loop(0, steps)
-    def _(step):
-        source = place(chip, chips, step, -1)
+    for head in ahead:
+        query_copy(head).start()
+    for other in packs_ahead:
+        gate_copy(other).start()
+
+    for source in behind:
         arrived(key_out, 2 * source + core, key_recv_sem.at[source])
         key_relay(source).start()
 
-    @pl.loop(0, steps)
-    def _(step):
-        source = place(chip, chips, step, -1)
+    for source in packs_ahead:
+        arrived(gate_recv, source, gate_recv_sem.at[source])
+    gate_half[core] = jnp.sum(gate_recv[...], axis=0)
+    half_copy = remote(
+        gate_half.at[core], gate_half.at[core], half_send_sem, half_recv_sem, partner
+    )
+    half_copy.start()
+
+    for source in behind:
         arrived(value_out, 2 * source + core, value_recv_sem.at[source])
         value_relay(source).start()
 
-    @pl.loop(0, steps)
-    def _(step):
-        source = place(chip, chips, step, -1)
-        arrived(query_out, source, query_recv_sem.at[source])
-        head = place(chip, chips, step, 1)
+    arrived(gate_half, 1 - core, half_recv_sem)
+    gate_out[...] = jnp.concatenate(
+        [gate_half[0, :, 0 : HD // 2], gate_half[1, :, 0 : HD // 2]], axis=1
+    )
+    half_copy.wait_send()
+    for other in packs_ahead:
+        gate_copy(other).wait_send()
+
+    own_query.wait()
+    for head in ahead:
         key_copy(head).wait_send()
         value_copy(head).wait_send()
         query_copy(head).wait_send()
-
-    @pl.loop(0, chips)
-    def _(source):
+    for source in behind:
+        arrived(query_out, source, query_recv_sem.at[source])
+
+    for source in behind + [chip]:
         tile = 2 * source + 1 - core
         arrived(key_out, tile, key_relay_recv_sem.at[source])
         arrived(value_out, tile, value_relay_recv_sem.at[source])
         key_relay(source).wait_send()
         value_relay(source).wait_send()
-
-
-def gate_kernel(packs, cond_ref, weight_ref, half_ref, send_buf, recv_buf, send_sem, recv_sem):
-    pack = lax.axis_index("dp")
-    barrier = pltpu.get_barrier_semaphore()
-
-    @pl.loop(1, packs)
-    def _(k):
-        other = {"dp": (pack + k) % packs}
-        pl.semaphore_signal(barrier, inc=1, device_id=other, device_id_type=MESH)
-
-    cond = cond_ref[...].astype(jnp.float32)
-    act = (cond / (1.0 + jnp.exp(-cond))).astype(jnp.bfloat16)
-    part = jnp.dot(act, weight_ref[...], preferred_element_type=jnp.float32)
-    send_buf[...] = jnp.zeros_like(send_buf)
-    for p in range(packs):
-        send_buf[p, 0:CLIPS, 0 : HD // 2] = part[p * CLIPS : (p + 1) * CLIPS, :]
-    recv_buf[pack] = send_buf[pack]
-
-    pl.semaphore_wait(barrier, packs - 1)
-
-    def gate_copy(other):
-        return remote(
-            send_buf.at[other],
-            recv_buf.at[pack],
-            send_sem.at[other],
-            recv_sem.at[pack],
-            {"dp": other},
-        )
-
-    @pl.loop(1, packs)
-    def _(k):
-        gate_copy((pack + k) % packs).start()
-
-    @pl.loop(1, packs)
-    def _(k):
-        source = (pack + packs - k) % packs
-        remote(
-            recv_buf.at[source],
-            recv_buf.at[source],
-            send_sem.at[source],
-            recv_sem.at[source],
-            {"dp": source},
-        ).wait_recv()
-
-    half_ref[...] = jnp.sum(recv_buf[...], axis=0)
-
-    @pl.loop(1, packs)
-    def _(k):
-        gate_copy((pack + k) % packs).wait_send()
 
 
 def attend_kernel(
@@ -241,8 +231,7 @@
     query_buf,
     key_buf,
     value_buf,
-    half_ref,
-    other_ref,
+    gate_ref,
     out_ref,
 ):
     seq = lax.axis_index("seq")
@@ -258,13 +247,7 @@
     rate = LOG2E / math.sqrt(HD)
     ones = jnp.ones((CHUNK * TILE, HD), jnp.bfloat16)
 
-    half = half_ref[:, 0 : HD // 2]
-    other_half = other_ref[:, 0 : HD // 2]
-    gates = jnp.where(
-        core == 0,
-        jnp.concatenate([half, other_half], axis=1),
-        jnp.concatenate([other_half, half], axis=1),
-    )
+    gates = gate_ref[...]
 
     def weigh(source):
         clip = clip_ref[0, 2 * source + core]
@@ -315,21 +298,21 @@
 
 def return_kernel(chips, attended_ref, out_ref, land_buf, send_sem, recv_sem, local_sem):
     seq = lax.axis_index("seq")
-    chip = seq // 2
-    core = seq % 2
+    chip = lax.div(seq, 2)
+    core = lax.rem(seq, 2)
     partner = {"seq": 2 * chip + 1 - core}
-    steps = chips - 1
+    ahead = others(chip, chips, 1)[::-1]
+    behind = others(chip, chips, -1)[::-1]
     barrier = pltpu.get_barrier_semaphore()
 
-    @pl.loop(1, chips)
-    def _(k):
-        other = {"seq": 2 * ((chip + k) % chips) + core}
-        pl.semaphore_signal(barrier, inc=1, device_id=other, device_id_type=MESH)
+    for other in behind:
+        device = {"seq": 2 * other + core}
+        pl.semaphore_signal(barrier, inc=1, device_id=device, device_id_type=MESH)
 
     own = pltpu.make_async_copy(attended_ref.at[chip], land_buf.at[chip], local_sem)
     own.start()
 
-    pl.semaphore_wait(barrier, steps)
+    pl.semaphore_wait(barrier, chips - 1)
 
     def out_copy(other):
         return remote(
@@ -340,28 +323,20 @@
             {"seq": 2 * other + core},
         )
 
-    @pl.loop(0, steps)
-    def _(step):
-        out_copy(place(chip, chips, chips - 2 - step, -1)).start()
+    for other in behind:
+        out_copy(other).start()
 
     own.wait()
     out_ref[:, columns(chip)] = land_buf[chip]
 
-    @pl.loop(0, steps)
-    def _(step):
-        head = place(chip, chips, chips - 2 - step, 1)
+    for head in ahead:
         remote(
-            land_buf.at[head],
-            land_buf.at[head],
-            send_sem.at[head],
-            recv_sem.at[head],
-            partner,
+            land_buf.at[head], land_buf.at[head], send_sem.at[head], recv_sem.at[head], partner
         ).wait_recv()
         out_ref[:, columns(head)] = land_buf[head]
 
-    @pl.loop(0, steps)
-    def _(step):
-        out_copy(place(chip, chips, step, -1)).wait_send()
+    for other in behind:
+        out_copy(other).wait_send()
 
 
 def per_device(query_rows, key_rows, value_rows, clip_tiles, conditioning, gate_weight):
@@ -376,41 +351,32 @@
     part_shape = jax.ShapeDtypeStruct((chips, TILE, HD), jnp.bfloat16)
     whole_shape = jax.ShapeDtypeStruct((2 * chips, TILE, HD), jnp.bfloat16)
 
-    half = pl.pallas_call(
-        functools.partial(gate_kernel, packs),
-        out_shape=jax.ShapeDtypeStruct((8, HD), jnp.float32),
-        in_specs=[vmem, vmem],
-        out_specs=vmem,
-        scratch_shapes=[
-            pltpu.VMEM((packs, 8, HD), jnp.float32),
-            pltpu.VMEM((packs, 8, HD), jnp.float32),
-            dma((packs,)),
-            dma((packs,)),
+    gate_buf = pltpu.VMEM((packs, 8, HD), jnp.float32)
+    query_all, key_all, value_all, gates = pl.pallas_call(
+        functools.partial(gather_kernel, chips, packs),
+        out_shape=[
+            part_shape,
+            whole_shape,
+            whole_shape,
+            jax.ShapeDtypeStruct((8, HD), jnp.float32),
         ],
-        compiler_params=pltpu.CompilerParams(collective_id=2, has_side_effects=True),
-        name="sum_gates",
-    )(conditioning, gate_weight)
-
-    other = lax.ppermute(half, "seq", [(i, i ^ 1) for i in range(seq_count)])
-
-    query_all, key_all, value_all = pl.pallas_call(
-        functools.partial(gather_kernel, chips),
-        out_shape=[part_shape, whole_shape, whole_shape],
-        in_specs=[anywhere] * 3,
-        out_specs=[anywhere] * 3,
-        scratch_shapes=[dma((chips,))] * 10 + [dma((3,))],
+        in_specs=[anywhere] * 3 + [vmem] * 2,
+        out_specs=[anywhere] * 3 + [vmem],
+        scratch_shapes=[gate_buf, gate_buf, pltpu.VMEM((2, 8, HD), jnp.float32)]
+        + [dma((chips,))] * 10
+        + [dma((3,)), dma((packs,)), dma((packs,)), dma, dma],
         compiler_params=pltpu.CompilerParams(collective_id=0, has_side_effects=True),
         name="gather_heads",
-    )(query_rows, key_rows, value_rows)
+    )(query_rows, key_rows, value_rows, conditioning, gate_weight.T)
 
     attended = pl.pallas_call(
         functools.partial(attend_kernel, chips, most),
         out_shape=part_shape,
-        in_specs=[smem, vmem, vmem, vmem, vmem, vmem],
+        in_specs=[smem, vmem, vmem, vmem, vmem],
         out_specs=vmem,
         compiler_params=pltpu.CompilerParams(vmem_limit_bytes=ATTEND_VMEM * 1024 * 1024),
         name="attend",
-    )(clip_tiles, query_all, key_all, value_all, half, other)
+    )(clip_tiles, query_all, key_all, value_all, gates)
 
     return pl.pallas_call(
         functools.partial(return_kernel, chips),

time: 107 us -> 88.3 us (0.83)
  Pallas kernels: 99.2 us -> 86.1 us
  starting transfers between devices: 3.75 us -> 0 us
  local copies, waits for them, and re-layouts: 3.9 us -> 1.88 us
    pallas_call x2 -> x1, Pallas kernels: 68.5 us -> 58.3 us  [per_device(): pl.pallas_call(functools.partial(gather_kernel, chips, packs), out_shape=...]
    ppermute x1 -> x0, starting transfers between devices: 3.75 us -> none  [per_device(): other = lax.ppermute(half, 'seq', [(i, i ^ 1) for i in range(seq_count)])]
    pallas_call x1, Pallas kernels: 22 us -> 19.1 us  [per_device(): pl.pallas_call(functools.partial(return_kernel, chips), out_shape=jax.Sha...]
    unnamed x4 -> x1, local copies, waits for them, and re-layouts: 3.9 us -> 1.88 us
  transfers between devices with their start and end apart: 1 -> 0, of which waited for: 0 -> 0; matrix products, arithmetic and copies ran while one was open for 0% -> 0% of each run, Pallas kernels for 39% -> 0%
where the time goes in v3:
time: 88.3 us; the launch traced here: 88 us
  Pallas kernels  86.1 us (98%)
  local copies, waits for them, and re-layouts  1.88 us (2%)
    pallas_call x1, Pallas kernels, per_device(): pl.pallas_call(functools.partial(gather_kernel, chips, packs), out_shape=...  58.3 us
    pallas_call x1, Pallas kernels, per_device(): pl.pallas_call(functools.partial(return_kernel, chips), out_shape=jax.Sha...  19.1 us
    pallas_call x1, Pallas kernels, per_device(): pl.pallas_call(functools.partial(attend_kernel, chips, most), out_shape=p...  8.64 us
    unnamed x1, local copies, waits for them, and re-layouts  1.88 us

profile of v3, /device:TPU:1, one launch (start us, length us, event | category | flops | bytes accessed | tf_op | source)
XLA Modules:
  0.0 88.0 jit_solution(5277711162151125114)
XLA Ops:
  0.0 58.3 %gather_heads.1 = (bf16[16,128,128]{2,1,0:T(8,128)(2,1)}, bf16[32,128,128]{2,1,0:T(8,128)(2,1)}, bf16[32,128,128]{2,1,0:T(8,128)(2,1)}, f32[8,128]{1,0:T(8,128)}) custom-call(bf16[128,2048]{1,0:T(8,128)(2,1)} %query_ref.1, bf16[128,2048]{1,0:T(8,128)(2,1)} %key_ref.1, bf16[128,2048]{1,0:T(8,128)(2,1)} %value_ref.1, bf16[96,128]{1,0:T(8,128)(2,1)} %cond_ref.1, ...), custom_call_target="tpu_custom_call" | custom-call | tf_op jit(solution)/shard_map/gather_heads/pallas_call | solution.py:355
  58.3 8.6 %attend.1.attended_ref = bf16[16,128,128]{2,1,0:T(8,128)(2,1)} custom-call(s32[1,32]{1,0:T(1,128)} %clip_ref.1, bf16[16,128,128]{2,1,0:T(8,128)(2,1)} %get-tuple-element.9.query_buf, bf16[32,128,128]{2,1,0:T(8,128)(2,1)} %get-tuple-element.10.key_buf, bf16[32,128,128]{2,1,0:T(8,128)(2,1)} %get-tuple-element.11.value_buf, f32[8,128]{1,0:T(8,128)} %get-tuple-element.12.gate_ref), custom_call_target="tpu_custom_call" | custom-call | tf_op jit(solution)/shard_map/attend/pallas_call | solution.py:372
  67.0 19.1 %return_tiles.1 = bf16[128,2048]{1,0:T(8,128)(2,1)} custom-call(bf16[16,128,128]{2,1,0:T(8,128)(2,1)} %attend.1.attended_ref), custom_call_target="tpu_custom_call" | custom-call | tf_op jit(solution)/shard_map/return_tiles/pallas_call | solution.py:381
  86.1 1.9 %copy.8 = bf16[128,2048]{1,0:T(8,128)(2,1)} copy(bf16[128,2048]{1,0:T(8,128)(2,1)} %return_tiles.1) | data formatting | bytes 1048576

commit v4 on v3

--- a/solution.py
+++ b/solution.py
@@ -12,7 +12,7 @@
 TILE = 128
 CLIPS = 4
 CHUNK = 2
-GROUP = 4
+GROUP = 8
 ATTEND_VMEM = 60
 LOG2E = 1.4426950408889634
 MESH = pl.DeviceIdType.MESH
@@ -83,8 +83,8 @@
     core = lax.rem(seq, 2)
     own_tile = seq
     partner = {"seq": 2 * chip + 1 - core}
-    ahead = others(chip, chips, 1)
-    behind = others(chip, chips, -1)
+    ahead = others(chip, chips, 1)[::-1]
+    behind = others(chip, chips, -1)[::-1]
     packs_ahead = [lax.rem(pack + k, packs) for k in range(1, packs)]
 
     barrier = pltpu.get_barrier_semaphore()
@@ -381,7 +381,7 @@
     return pl.pallas_call(
         functools.partial(return_kernel, chips),
         out_shape=jax.ShapeDtypeStruct(query_rows.shape, jnp.bfloat16),
-        in_specs=[anywhere],
+        in_specs=[pl.BlockSpec(memory_space=pltpu.HBM)],
         out_specs=vmem,
         scratch_shapes=[
             pltpu.VMEM((chips, TILE, HD), jnp.bfloat16),
@@ -389,7 +389,9 @@
             dma((chips,)),
             dma,
         ],
-        compiler_params=pltpu.CompilerParams(collective_id=1, has_side_effects=True),
+        compiler_params=pltpu.CompilerParams(
+            collective_id=1, has_side_effects=True, vmem_limit_bytes=16 * 1024 * 1024
+        ),
         name="return_tiles",
     )(attended)
 

time: 88.3 us -> 88.4 us (level)
    unnamed x1 -> x3, local copies, waits for them, and re-layouts: 1.88 us -> 1.84 us
where the time goes in v4:
time: 88.4 us; the launch traced here: 88.1 us
  Pallas kernels  86.3 us (98%)
  local copies, waits for them, and re-layouts  1.84 us (2%)
    pallas_call x1, Pallas kernels, per_device(): pl.pallas_call(functools.partial(gather_kernel, chips, packs), out_shape=...  58 us
    pallas_call x1, Pallas kernels, per_device(): pl.pallas_call(functools.partial(return_kernel, chips), out_shape=jax.Sha...  19.9 us
    pallas_call x1, Pallas kernels, per_device(): pl.pallas_call(functools.partial(attend_kernel, chips, most), out_shape=p...  8.3 us
    unnamed x3, local copies, waits for them, and re-layouts  1.84 us

profile of v4, /device:TPU:1, one launch (start us, length us, event | category | flops | bytes accessed | tf_op | source)
XLA Modules:
  0.0 88.1 jit_solution(13815882668377381878)
XLA Ops:
  0.0 58.0 %gather_heads.1 = (bf16[16,128,128]{2,1,0:T(8,128)(2,1)}, bf16[32,128,128]{2,1,0:T(8,128)(2,1)}, bf16[32,128,128]{2,1,0:T(8,128)(2,1)}, f32[8,128]{1,0:T(8,128)}) custom-call(bf16[128,2048]{1,0:T(8,128)(2,1)} %query_ref.1, bf16[128,2048]{1,0:T(8,128)(2,1)} %key_ref.1, bf16[128,2048]{1,0:T(8,128)(2,1)} %value_ref.1, bf16[96,128]{1,0:T(8,128)(2,1)} %cond_ref.1, ...), custom_call_target="tpu_custom_call" | custom-call | tf_op jit(solution)/shard_map/gather_heads/pallas_call | solution.py:355
  58.0 8.3 %attend.1.attended_ref = bf16[16,128,128]{2,1,0:T(8,128)(2,1)} custom-call(s32[1,32]{1,0:T(1,128)} %clip_ref.1, bf16[16,128,128]{2,1,0:T(8,128)(2,1)} %get-tuple-element.9.query_buf, bf16[32,128,128]{2,1,0:T(8,128)(2,1)} %get-tuple-element.10.key_buf, bf16[32,128,128]{2,1,0:T(8,128)(2,1)} %get-tuple-element.11.value_buf, f32[8,128]{1,0:T(8,128)} %get-tuple-element.12.gate_ref), custom_call_target="tpu_custom_call" | custom-call | tf_op jit(solution)/shard_map/attend/pallas_call | solution.py:372
  66.3 0.0 copy-start
  66.3 1.0 %copy-done = bf16[16,128,128]{2,1,0:T(8,128)(2,1)S(1)} copy-done((bf16[16,128,128]{2,1,0:T(8,128)(2,1)S(1)}, bf16[16,128,128]{2,1,0:T(8,128)(2,1)}, u32[]{:S(2)}) %copy-start) | copy-done | bytes 524312
  67.4 19.9 %return_tiles.1 = bf16[128,2048]{1,0:T(8,128)(2,1)S(1)} custom-call(bf16[16,128,128]{2,1,0:T(8,128)(2,1)S(1)} %copy-done), custom_call_target="tpu_custom_call" | custom-call | tf_op jit(solution)/shard_map/return_tiles/pallas_call | solution.py:381
  87.3 0.8 copy.8
Async XLA Ops:
  66.3 1.0 %copy-start = (bf16[16,128,128]{2,1,0:T(8,128)(2,1)S(1)}, bf16[16,128,128]{2,1,0:T(8,128)(2,1)}, u32[]{:S(2)}) copy-start(bf16[16,128,128]{2,1,0:T(8,128)(2,1)} %attend.1.attended_ref) | copy-start | bytes 1572868

commit v5 on v4

--- a/solution.py
+++ b/solution.py
@@ -83,8 +83,8 @@
     core = lax.rem(seq, 2)
     own_tile = seq
     partner = {"seq": 2 * chip + 1 - core}
-    ahead = others(chip, chips, 1)[::-1]
-    behind = others(chip, chips, -1)[::-1]
+    ahead = others(chip, chips, 1)
+    behind = others(chip, chips, -1)
     packs_ahead = [lax.rem(pack + k, packs) for k in range(1, packs)]
 
     barrier = pltpu.get_barrier_semaphore()

time: 88.4 us -> 86.9 us (0.983)
  Pallas kernels: 86.3 us -> 84.8 us
    pallas_call x1, Pallas kernels: 19.9 us -> 18.2 us  [per_device(): pl.pallas_call(functools.partial(return_kernel, chips), out_shape=jax.Sha...]
where the time goes in v5:
time: 86.9 us; the launch traced here: 86.6 us
  Pallas kernels  84.8 us (98%)
  local copies, waits for them, and re-layouts  1.84 us (2%)
    pallas_call x1, Pallas kernels, per_device(): pl.pallas_call(functools.partial(gather_kernel, chips, packs), out_shape=...  58.3 us
    pallas_call x1, Pallas kernels, per_device(): pl.pallas_call(functools.partial(return_kernel, chips), out_shape=jax.Sha...  18.2 us
    pallas_call x1, Pallas kernels, per_device(): pl.pallas_call(functools.partial(attend_kernel, chips, most), out_shape=p...  8.3 us
    unnamed x3, local copies, waits for them, and re-layouts  1.84 us

profile of v5, /device:TPU:1, one launch (start us, length us, event | category | flops | bytes accessed | tf_op | source)
XLA Modules:
  0.0 86.6 jit_solution(10059874458245608100)
XLA Ops:
  0.0 58.3 %gather_heads.1 = (bf16[16,128,128]{2,1,0:T(8,128)(2,1)}, bf16[32,128,128]{2,1,0:T(8,128)(2,1)}, bf16[32,128,128]{2,1,0:T(8,128)(2,1)}, f32[8,128]{1,0:T(8,128)}) custom-call(bf16[128,2048]{1,0:T(8,128)(2,1)} %query_ref.1, bf16[128,2048]{1,0:T(8,128)(2,1)} %key_ref.1, bf16[128,2048]{1,0:T(8,128)(2,1)} %value_ref.1, bf16[96,128]{1,0:T(8,128)(2,1)} %cond_ref.1, ...), custom_call_target="tpu_custom_call" | custom-call | tf_op jit(solution)/shard_map/gather_heads/pallas_call | solution.py:355
  58.3 8.3 %attend.1.attended_ref = bf16[16,128,128]{2,1,0:T(8,128)(2,1)} custom-call(s32[1,32]{1,0:T(1,128)} %clip_ref.1, bf16[16,128,128]{2,1,0:T(8,128)(2,1)} %get-tuple-element.9.query_buf, bf16[32,128,128]{2,1,0:T(8,128)(2,1)} %get-tuple-element.10.key_buf, bf16[32,128,128]{2,1,0:T(8,128)(2,1)} %get-tuple-element.11.value_buf, f32[8,128]{1,0:T(8,128)} %get-tuple-element.12.gate_ref), custom_call_target="tpu_custom_call" | custom-call | tf_op jit(solution)/shard_map/attend/pallas_call | solution.py:372
  66.6 0.0 copy-start
  66.6 1.0 %copy-done = bf16[16,128,128]{2,1,0:T(8,128)(2,1)S(1)} copy-done((bf16[16,128,128]{2,1,0:T(8,128)(2,1)S(1)}, bf16[16,128,128]{2,1,0:T(8,128)(2,1)}, u32[]{:S(2)}) %copy-start) | copy-done | bytes 524312
  67.7 18.2 %return_tiles.1 = bf16[128,2048]{1,0:T(8,128)(2,1)S(1)} custom-call(bf16[16,128,128]{2,1,0:T(8,128)(2,1)S(1)} %copy-done), custom_call_target="tpu_custom_call" | custom-call | tf_op jit(solution)/shard_map/return_tiles/pallas_call | solution.py:381
  85.8 0.8 copy.8
Async XLA Ops:
  66.6 1.0 %copy-start = (bf16[16,128,128]{2,1,0:T(8,128)(2,1)S(1)}, bf16[16,128,128]{2,1,0:T(8,128)(2,1)}, u32[]{:S(2)}) copy-start(bf16[16,128,128]{2,1,0:T(8,128)(2,1)} %attend.1.attended_ref) | copy-start | bytes 1572868
